TPU v7x, 32 devices: a whole 2x2x4 slice. The times are simulated.
32 devices in a mesh: groups: 2 (over x), tensor: 8 (over z, y), section: 2 (over core).
Axes of the slice: x: 2, y: 2, z: 4, core: 2. Of those that a mesh axis runs over, the one named last changes fastest.
Arguments:
- prefill_queries: bfloat16 [2, 4096, 8192], P('section', ('groups', 'tensor')), parts along dimension 1, may hold values from -26 to 26
- prefill_key_values: bfloat16 [2, 4096, 2048], P('section', ('groups', 'tensor')), parts along dimension 1, may hold values from -6 to 6
- decode_step_queries: bfloat16 [256, 8192], P(('groups', 'tensor', 'section')), parts along dimension 0, may hold values from -26 to 26
- cached_page_pool: bfloat16 [2048, 4, 2048], P(('groups', 'tensor', 'section')), parts along dimension 0, may hold values from -6 to 6
- trajectory_page_table: int32 [256, 8], P(('groups', 'tensor', 'section')), parts along dimension 0, may hold values from 0 to 63, as said below
- lengths: int32 [256], P(('groups', 'tensor', 'section')), parts along dimension 0, may hold values from 2 to 32, as said below
- page_owner: int32 [2, 1024], P(None, 'groups'), parts along dimension 1, may hold values from 0 to 15, as said below
- page_slot: int32 [2, 1024], P(None, 'groups'), parts along dimension 1, may hold values from 0 to 7
Outputs:
- stretch_context: bfloat16 [2, 4096, 8192], P('section', ('groups', 'tensor')), parts along dimension 1
- step_context: bfloat16 [256, 8192], P(('groups', 'tensor', 'section')), parts along dimension 0
There are 2 independent parts, one for each index of `groups`. A program takes and returns all parts, laid end to end along the dimension named above; each array names one. Nothing has to cross between parts.
Inputs may be any that keep to these rules, and one draw needn't show every extreme that they name: `page_owner`: cut each stretch's 512 pages into blocks of 512 consecutive pages: no owner is named by more than 64 pages of one block, and one owner is named by exactly 64 pages of every block. `trajectory_page_table`: the rows of the 8 trajectories of one owner together name each of its 64 slots exactly once. `lengths`: every owner has a trajectory of length 32.
All inputs are finite; a program needn't handle non-finite values.
Results may differ from a plain program's by a relative error of at most 0.004.
Values may be sent and summed in bfloat16 or wider, within the bound.
A program may use at most 320 MiB of HBM per device.

v0:
```python
import math

import jax
import jax.numpy as jnp
from jax import lax
from jax.sharding import PartitionSpec as P

QUERY_HEADS = 64
KEY_VALUE_HEADS = 8
HEAD_SIZE = 128
PAGE_TOKENS = 4


def on_device(
    prefill_queries,
    prefill_key_values,
    decode_step_queries,
    cached_page_pool,
    trajectory_page_table,
    lengths,
    page_owner,
    page_slot,
):
    tensor_total = lax.axis_size("tensor")
    section_total = lax.axis_size("section")
    tensor_position = lax.axis_index("tensor")
    section_index = lax.axis_index("section")
    quarter_pieces = tensor_total // KEY_VALUE_HEADS
    key_value_head = tensor_position % KEY_VALUE_HEADS
    quarter_piece = tensor_position // KEY_VALUE_HEADS
    owner_local_rows = prefill_queries.shape[1]
    portion_rows = owner_local_rows // quarter_pieces
    stretch_rows = owner_local_rows * tensor_total
    query_group_size = QUERY_HEADS // KEY_VALUE_HEADS
    head_size_value = query_group_size * HEAD_SIZE
    key_value_width = 2 * HEAD_SIZE
    scaling = 1.0 / math.sqrt(HEAD_SIZE)
    query_vectors = prefill_queries.reshape(
        portion_rows, quarter_pieces * KEY_VALUE_HEADS, head_size_value
    )
    key_value_rows = prefill_key_values.reshape(owner_local_rows, KEY_VALUE_HEADS * key_value_width)
    own_queries = lax.all_to_all(query_vectors, "tensor", split_axis=1, concat_axis=0, tiled=True)
    head_rows = lax.dynamic_slice_in_dim(
        lax.all_gather(key_value_rows, "tensor", axis=0, tiled=True),
        key_value_head * key_value_width,
        key_value_width,
        1,
    )
    row_count = tensor_total * portion_rows
    own_queries = own_queries.reshape(row_count, query_group_size, HEAD_SIZE)
    row_ids = jnp.arange(row_count, dtype=jnp.int32)
    positions = (
        row_ids // portion_rows * owner_local_rows
        + row_ids % portion_rows * quarter_pieces
        + quarter_piece
    )
    causal = positions[:, None] >= jnp.arange(stretch_rows, dtype=jnp.int32)[None, :]
    key_part = head_rows[:, :HEAD_SIZE]
    value_part = head_rows[:, HEAD_SIZE:]
    outputs = []
    for member in range(query_group_size):
        scores = (
            jnp.einsum(
                "rd,nd->rn", own_queries[:, member], key_part, preferred_element_type=jnp.float32
            )
            * scaling
        )
        scores = jnp.where(causal, scores, -jnp.inf)
        row_top = jnp.max(scores, axis=1, keepdims=True)
        exp_terms = jnp.exp(scores - row_top)
        totals = jnp.sum(exp_terms, axis=1, keepdims=True)
        mixture = (
            jnp.dot(exp_terms.astype(jnp.bfloat16), value_part, preferred_element_type=jnp.float32)
            / totals
        )
        outputs.append(mixture)
    attended = (
        jnp.stack(outputs, axis=1)
        .astype(jnp.bfloat16)
        .reshape(tensor_total, portion_rows, 1, head_size_value)
    )
    returned = lax.all_to_all(attended, "tensor", split_axis=0, concat_axis=2, tiled=True)
    stretch_context = returned.reshape(owner_local_rows, QUERY_HEADS * HEAD_SIZE)[None]
    owners = tensor_total * section_total
    pages_block = stretch_rows // PAGE_TOKENS // quarter_pieces
    slot_capacity = 2 * pages_block // owners
    owner_rows = page_owner.reshape(section_total, quarter_pieces, pages_block)
    slot_rows = page_slot.reshape(section_total, quarter_pieces, pages_block)
    own_pages = lax.dynamic_slice_in_dim(
        head_rows, quarter_piece * pages_block * PAGE_TOKENS, pages_block * PAGE_TOKENS, 0
    )
    own_pages = own_pages.reshape(pages_block, PAGE_TOKENS * key_value_width)
    block_owner = owner_rows[section_index, quarter_piece]
    onehot = (block_owner[:, None] == jnp.arange(owners, dtype=jnp.int32)[None, :]).astype(
        jnp.int32
    )
    before = jnp.cumsum(onehot, axis=0) - onehot
    page_rank = jnp.sum(before * onehot, axis=1)
    select = (jnp.transpose(onehot)[:, None, :] == 1) & (
        page_rank[None, None, :] == jnp.arange(slot_capacity, dtype=jnp.int32)[None, :, None]
    )
    outgoing = jnp.einsum(
        "ocp,px->ocx", select.astype(jnp.bfloat16), own_pages, preferred_element_type=jnp.float32
    )
    outgoing = outgoing.astype(jnp.bfloat16).reshape(
        owners, slot_capacity, PAGE_TOKENS, key_value_width
    )
    incoming_pages = lax.all_to_all(
        outgoing, ("tensor", "section"), split_axis=0, concat_axis=0, tiled=True
    )
    fresh_rows = incoming_pages.reshape(
        quarter_pieces, KEY_VALUE_HEADS, section_total, slot_capacity, PAGE_TOKENS, 2, HEAD_SIZE
    )
    fresh_rows = jnp.transpose(fresh_rows, (2, 0, 3, 4, 1, 5, 6)).reshape(
        section_total * quarter_pieces * slot_capacity * PAGE_TOKENS, KEY_VALUE_HEADS, 2, HEAD_SIZE
    )
    own_owner = tensor_position * section_total + section_index
    is_mine = (owner_rows == own_owner).astype(jnp.int32)
    before_mine = jnp.cumsum(is_mine, axis=2) - is_mine
    landed = (is_mine[:, :, None, :] == 1) & (
        before_mine[:, :, None, :]
        == jnp.arange(slot_capacity, dtype=jnp.int32)[None, None, :, None]
    )
    slot_of = jnp.sum(jnp.where(landed, slot_rows[:, :, None, :], 0), axis=-1)
    filled = jnp.any(landed, axis=-1)
    new_target = jnp.where(filled, slot_of, -1).reshape(
        section_total * quarter_pieces * slot_capacity
    )
    trajectory_total = decode_step_queries.shape[0]
    new_mask = (
        jnp.repeat(new_target, PAGE_TOKENS)[None, :]
        == jnp.arange(trajectory_total, dtype=jnp.int32)[:, None]
    )
    decode_step_rows = decode_step_queries.reshape(
        trajectory_total, KEY_VALUE_HEADS, query_group_size, HEAD_SIZE
    )
    previous_extent = trajectory_page_table.shape[1] * PAGE_TOKENS
    previous_rows = cached_page_pool[trajectory_page_table].reshape(
        trajectory_total, previous_extent, KEY_VALUE_HEADS, 2, HEAD_SIZE
    )
    old_mask = jnp.arange(previous_extent, dtype=jnp.int32)[None, :] < lengths[:, None]
    old_scores = (
        jnp.einsum(
            "tkgd,tnkd->tkgn",
            decode_step_rows,
            previous_rows[:, :, :, 0],
            preferred_element_type=jnp.float32,
        )
        * scaling
    )
    old_scores = jnp.where(old_mask[:, None, None, :], old_scores, -jnp.inf)
    new_scores = (
        jnp.einsum(
            "tkgd,nkd->tkgn",
            decode_step_rows,
            fresh_rows[:, :, 0],
            preferred_element_type=jnp.float32,
        )
        * scaling
    )
    new_scores = jnp.where(new_mask[:, None, None, :], new_scores, -jnp.inf)
    row_top = jnp.maximum(jnp.max(old_scores, axis=-1), jnp.max(new_scores, axis=-1))[..., None]
    old_terms = jnp.exp(old_scores - row_top)
    new_terms = jnp.exp(new_scores - row_top)
    totals = jnp.sum(old_terms, axis=-1) + jnp.sum(new_terms, axis=-1)
    mixture = jnp.einsum(
        "tkgn,tnkd->tkgd",
        old_terms.astype(jnp.bfloat16),
        previous_rows[:, :, :, 1],
        preferred_element_type=jnp.float32,
    )
    mixture = mixture + jnp.einsum(
        "tkgn,nkd->tkgd",
        new_terms.astype(jnp.bfloat16),
        fresh_rows[:, :, 1],
        preferred_element_type=jnp.float32,
    )
    mixture = mixture / totals[..., None]
    step_context = mixture.reshape(trajectory_total, QUERY_HEADS * HEAD_SIZE).astype(jnp.bfloat16)
    return (stretch_context, step_context)


def solution(mesh):
    placed = (
        P("section", ("groups", "tensor"), None),
        P("section", ("groups", "tensor"), None),
        P(("groups", "tensor", "section"), None),
        P(("groups", "tensor", "section"), None, None),
        P(("groups", "tensor", "section"), None),
        P(("groups", "tensor", "section")),
        P(None, "groups"),
        P(None, "groups"),
    )
    return jax.shard_map(
        on_device,
        mesh=mesh,
        in_specs=placed,
        out_specs=(
            P("section", ("groups", "tensor"), None),
            P(("groups", "tensor", "section"), None),
        ),
        check_vma=False,
    )
```

profile of v0, /device:TPU:29, one launch (start us, length us, event | category | flops | bytes accessed | tf_op | source)
XLA Modules:
  0.0 560.2 jit_solution(7868399660400718628)
XLA Ops:
  7.2 0.7 all-gather.3.cloned.1.call-update
  7.9 6.5 %copy.99 = bf16[32,8,8,1024]{3,2,1,0:T(8,128)(2,1)S(1)} copy(bf16[32,8,8,1024]{3,1,2,0:T(8,128)(2,1)} %bitcast.299) | data formatting | bytes 8388608
  14.4 4.3 copy.71
  18.8 5.7 %all-to-all-start = ((bf16[256,8,1024]{2,0,1:T(8,128)(2,1)}), bf16[256,8,1024]{2,0,1:T(8,128)(2,1)}, u32[]{:S(2)}, u32[]{:S(2)}) async-start(bf16[256,8,1024]{2,0,1:T(8,128)(2,1)} %copy.71), calls=%async_computation | async-start | bytes 8388608 | tf_op jit(solution)/shard_map/all_to_all | solution.py:42
  24.6 1.2 reduce-window.16
  25.7 0.2 slice_reduce_fusion
  26.0 0.1 fusion.203
  26.1 171.7 %all-to-all-done = bf16[256,8,1024]{2,0,1:T(8,128)(2,1)} async-done(((bf16[256,8,1024]{2,0,1:T(8,128)(2,1)}), bf16[256,8,1024]{2,0,1:T(8,128)(2,1)}, u32[]{:S(2)}, u32[]{:S(2)}) %all-to-all-start) | async-done | bytes 4194336 | tf_op jit(solution)/shard_map/all_to_all | solution.py:42
  197.8 3.3 copy.100
  201.1 8.2 %fusion.232 = (bf16[2048,1,128]{2,1,0:T(2,128)(2,1)}, bf16[2048,1,128]{2,1,0:T(2,128)(2,1)}, bf16[2048,1,128]{2,1,0:T(2,128)(2,1)}, bf16[2048,1,128]{2,1,0:T(2,1...) fusion(bf16[2048,8,128]{2,1,0:T(8,128)(2,1)S(1)} %bitcast.295), kind=kLoop, calls=%fused_computation.215 | loop fusion | bytes 8388608 | tf_op jit(solution)/shard_map/slice | solution.py:64
  209.2 4.4 all-gather.3.cloned.1.call-done
  213.6 1.3 constant_dynamic-slice_fusion.1
  214.9 1.4 reshape.294
  216.3 3.8 fusion.138
  220.1 4.5 reshape.277
  224.7 7.4 %all-to-all-start.2 = ((bf16[16,64,4,256]{3,2,1,0:T(4,128)(2,1)}), bf16[16,64,4,256]{3,2,1,0:T(4,128)(2,1)}, u32[]{:S(2)}, u32[]{:S(2)}) async-start(bf16[16,64,4,256]{3,2,1,0:T(4,128)(2,1)} %reshape.277), calls=%async_computation.2 | async-start | bytes 4194304 | tf_op jit(solution)/shard_map/all_to_all | solution.py:108
  232.1 1.4 fusion.237
  233.5 9.4 %fusion.170 = f32[2048,2048]{1,0:T(8,128)} fusion(bf16[2048,1,128]{2,1,0:T(2,128)(2,1)} %get-tuple-element.28, bf16[2048,256]{1,0:T(8,128)(2,1)S(1)} %fusion.237), kind=kOutput, calls=%fused_computation.123 | convolution fusion | flops 1073741824 | bytes 17825792 | tf_op jit(solution)/shard_map/rd,nd->rn/dot_general | solution.py:63
  242.8 8.1 %fusion.158 = f32[2048,2048]{1,0:T(8,128)} fusion(bf16[2048,1,128]{2,1,0:T(2,128)(2,1)S(1)} %copy-done.5, bf16[2048,256]{1,0:T(8,128)(2,1)S(1)} %fusion.237), kind=kOutput, calls=%fused_computation.111 | convolution fusion | flops 1073741824 | bytes 18350080 | tf_op jit(solution)/shard_map/rd,nd->rn/dot_general | solution.py:63
  250.9 8.1 %fusion.161 = f32[2048,2048]{1,0:T(8,128)} fusion(bf16[2048,1,128]{2,1,0:T(2,128)(2,1)S(1)} %copy-done.4, bf16[2048,256]{1,0:T(8,128)(2,1)S(1)} %fusion.237), kind=kOutput, calls=%fused_computation.114 | convolution fusion | flops 1073741824 | bytes 18350080 | tf_op jit(solution)/shard_map/rd,nd->rn/dot_general | solution.py:63
  259.0 8.1 %fusion.164 = f32[2048,2048]{1,0:T(8,128)} fusion(bf16[2048,1,128]{2,1,0:T(2,128)(2,1)S(1)} %copy-done.3, bf16[2048,256]{1,0:T(8,128)(2,1)S(1)} %fusion.237), kind=kOutput, calls=%fused_computation.117 | convolution fusion | flops 1073741824 | bytes 18350080 | tf_op jit(solution)/shard_map/rd,nd->rn/dot_general | solution.py:63
  267.1 8.1 %fusion.167 = f32[2048,2048]{1,0:T(8,128)} fusion(bf16[2048,1,128]{2,1,0:T(2,128)(2,1)S(1)} %copy-done.2, bf16[2048,256]{1,0:T(8,128)(2,1)S(1)} %fusion.237), kind=kOutput, calls=%fused_computation.120 | convolution fusion | flops 1073741824 | bytes 18350080 | tf_op jit(solution)/shard_map/rd,nd->rn/dot_general | solution.py:63
  275.2 2.8 fusion.173
  278.1 10.7 %fusion.23 = (f32[2048]{0:T(1024)S(1)}, f32[2048]{0:T(1024)S(1)}, f32[2048,2048]{1,0:T(8,128)}) fusion(s32[2048]{0:T(1024)S(1)} %fusion.213, f32[2048,2048]{1,0:T(8,128)S(1)} %fusion.173, bf16[2048,1,128]{2,1,0:T(2,128)(2,1)} %get-tuple-element.29, bf16[2048,256]{1,0:T(8,128)(2,1)S(1)} %fusion.237), kind=kOutput, calls=%fused_computation.41 | convolution fusion | flops 1103097856 | bytes 34627584 | tf_op jit(solution)/shard_map/rd,nd->rn/dot_general | solution.py:63
  288.8 0.6 copy-done.1
  289.4 45.0 %fusion.14 = (f32[2048]{0:T(1024)S(1)}, f32[2048]{0:T(1024)S(1)}, f32[2048]{0:T(1024)S(1)}, f32[2048]{0:T(1024)S(1)}, f32[2048]{0:T(1024)S(1)}, /*index=5*/f32[2...) fusion(f32[2048,2048]{1,0:T(8,128)} %get-tuple-element.40, f32[2048]{0:T(1024)S(1)} %get-tuple-element.18, ...), kind=kOutput, calls=%fused_computation.32 | convolution fusion | flops 1186971648 | bytes 135880704 | tf_op jit(solution)/shard_map/rd,nd->rn/dot_general | solution.py:63
  334.4 8.6 %fusion.51 = bf16[2048,8,128]{2,0,1:T(8,128)(2,1)} fusion(f32[2048,2048]{1,0:T(8,128)} %copy-done.1, f32[2048]{0:T(1024)S(1)} %get-tuple-element.19, s32[2048]{0:T(1024)S(1)} %fusion.213, f32[2048]{0:T(1024)S(1)} %get-tuple-element.17, bf16[2048,256]{1,0:T(8,128)(2,1)S(1)} %fusion.237), kind=kOutput, calls=%fused_computation.55 | convolution fusion | flops 1095237632 | bytes 17850368 | tf_op jit(solution)/shard_map/dot_general | solution.py:73
  343.0 35.7 %fusion.12 = (f32[2048]{0:T(1024)S(1)}, f32[2048]{0:T(1024)S(1)}, f32[2048]{0:T(1024)S(1)}, f32[2048]{0:T(1024)S(1)}, f32[2048]{0:T(1024)S(1)}, /*index=5*/f32[2048]{0:T(1024)S(1)}) fusion(f32[2048,2048]{1,0:T(8,128)} %get-tuple-element.41, f32[2048]{0:T(1024)S(1)} %get-tuple-element.11, s32[2048]{0:T(1024)S(1)} %fusion.213, f32[2048]{0:T(1024)S(1)} %get-tuple-element.16, ...), kind=kLoop, calls=%fused_computation.30 | loop fusion | flops 104845312 | bytes 100769792 | tf_op jit(solution)/shard_map/reduce_sum | solution.py:71
  378.8 8.8 %fusion.63 = bf16[2048,8,128]{2,0,1:T(8,128)(2,1)} fusion(bf16[2048,8,128]{2,0,1:T(8,128)(2,1)} %fusion.51, f32[2048,2048]{1,0:T(8,128)} %fusion.170, f32[2048]{0:T(1024)S(1)} %get-tuple-element.16, s32[2048]{0:T(1024)S(1)} %fusion.213, f32[2048]{0:T(1024)S(1)} %get-tuple-element.21, bf16[2048,256]{1,0:T(8,128)(2,1)S(1)} %fusion.237), kind=kOutput, calls=%fused_computation.59 | convolution fusion | flops 1095237632 | bytes 17850368 | tf_op jit(solution)/shard_map/dot_general | solution.py:73
  387.5 8.8 %fusion.75 = bf16[2048,8,128]{2,0,1:T(8,128)(2,1)} fusion(bf16[2048,8,128]{2,0,1:T(8,128)(2,1)} %fusion.63, f32[2048,2048]{1,0:T(8,128)} %fusion.167, f32[2048]{0:T(1024)S(1)} %get-tuple-element.15, s32[2048]{0:T(1024)S(1)} %fusion.213, f32[2048]{0:T(1024)S(1)} %get-tuple-element.22, bf16[2048,256]{1,0:T(8,128)(2,1)S(1)} %fusion.237), kind=kOutput, calls=%fused_computation.63 | convolution fusion | flops 1095237632 | bytes 17850368 | tf_op jit(solution)/shard_map/dot_general | solution.py:73
  396.4 5.3 fusion.87
  401.6 8.8 %fusion.99 = bf16[2048,8,128]{2,0,1:T(8,128)(2,1)} fusion(bf16[2048,8,128]{2,0,1:T(8,128)(2,1)} %fusion.87, f32[2048,2048]{1,0:T(8,128)} %fusion.161, f32[2048]{0:T(1024)S(1)} %get-tuple-element.13, s32[2048]{0:T(1024)S(1)} %fusion.213, f32[2048]{0:T(1024)S(1)} %get-tuple-element.24, bf16[2048,256]{1,0:T(8,128)(2,1)S(1)} %fusion.237), kind=kOutput, calls=%fused_computation.71 | convolution fusion | flops 1095237632 | bytes 17850368 | tf_op jit(solution)/shard_map/dot_general | solution.py:73
  410.4 5.0 fusion.111
  415.5 8.8 %fusion.123 = bf16[2048,8,128]{2,0,1:T(8,128)(2,1)} fusion(bf16[2048,8,128]{2,0,1:T(8,128)(2,1)} %fusion.111, f32[2048,2048]{1,0:T(8,128)} %get-tuple-element.41, f32[2048]{0:T(1024)S(1)} %get-tuple-element.11, s32[2048]{0:T(1024)S(1)} %fusion.213, f32[2048]{0:T(1024)S(1)} %get-tuple-element.20, bf16[2048,256]{1,0:T(8,128)(2,1)S(1)} %fusion.237), kind=kOutput, calls=%fused_computation.79 | convolution fusion | flops 1095237632 | bytes 17850368 | tf_op jit(solution)/shard_map/dot_general | solution.py:73
  424.3 5.0 fusion.135
  429.3 6.4 %copy.72 = bf16[2048,8,128]{2,1,0:T(8,128)(2,1)} copy(bf16[2048,8,128]{2,0,1:T(8,128)(2,1)} %fusion.135) | data formatting | bytes 8388608 | tf_op jit(solution)/shard_map/stack | solution.py:78
  435.7 7.3 %convert_element_type.77 = bf16[8,256,1,1024]{3,1,0,2:T(8,128)(2,1)} reshape(bf16[2048,8,128]{2,1,0:T(8,128)(2,1)} %copy.72) | data formatting | bytes 8388608 | tf_op jit(solution)/shard_map/convert_element_type | solution.py:79
  443.0 5.4 all-to-all-start.1
  448.4 0.1 reshape.282
  448.6 0.6 reduce-window.14
  449.2 0.2 slice_reduce_fusion.1
  449.4 0.2 reduce-window.15
  449.6 0.1 broadcast_bitcast_fusion
  449.7 0.1 fusion.178
  449.8 0.2 select_reduce_fusion
  450.0 0.1 select_n.117
  450.1 0.1 broadcast_in_dim.96
  450.1 0.1 eq.136
  450.3 1.4 gather_fusion
  451.7 0.7 reshape.268
  452.5 0.1 iota_compare_fusion.7
  452.5 2.3 fusion.233
  454.9 1.4 fusion.234
  456.2 2.8 reshape.278
  459.0 1.0 copy.79
  460.0 1.5 fusion.235
  461.5 0.3 fusion.179
  461.7 0.3 fusion.150
  462.1 0.3 convolution_bitcast_fusion
  462.4 1.6 fusion.147
  464.0 0.7 copy.163
  464.7 75.4 %all-to-all-done.1 = bf16[8,256,1,1024]{3,1,2,0:T(8,128)(2,1)} async-done(((bf16[8,256,1,1024]{3,1,2,0:T(8,128)(2,1)}), bf16[8,256,1,1024]{3,1,2,0:T(8,128)(2,1)}, u32[]{:S(2)}, u32[]{:S(2)}) %all-to-all-start.1) | async-done | bytes 4194336 | tf_op jit(solution)/shard_map/all_to_all | solution.py:82
  540.1 6.4 %copy.74 = bf16[8,256,1,1024]{1,3,0,2:T(8,128)(2,1)} copy(bf16[8,256,1,1024]{3,1,2,0:T(8,128)(2,1)} %all-to-all-done.1) | data formatting | bytes 8388608 | tf_op jit(solution)/shard_map/all_to_all | solution.py:82
  546.6 6.3 %copy.86 = bf16[1,256,8192]{2,1,0:T(8,128)(2,1)} copy(bf16[1,256,8192]{1,2,0:T(8,128)(2,1)} %bitcast.297) | data formatting | bytes 8388608
  (70 shorter events, 0.3 us)
Async XLA Ops:
  7.2 443.1 %copy-start = (bf16[64,4,2048]{2,1,0:T(4,128)(2,1)S(1)}, bf16[64,4,2048]{2,1,0:T(4,128)(2,1)}, u32[]{:S(2)}) copy-start(bf16[64,4,2048]{2,1,0:T(4,128)(2,1)} %param.11) | copy-start | bytes 3145732
  7.2 17.3 %copy-start.7 = (s32[2,512]{1,0:T(2,128)S(1)}, s32[2,512]{1,0:T(2,128)}, u32[]{:S(2)}) copy-start(s32[2,512]{1,0:T(2,128)} %param.14) | copy-start | bytes 12292
  7.2 206.4 %all-gather.3.cloned.1.call-start = ((), (), s32[]{:S(2)}) async-start(), calls=%async_computation.3 | async-start | bytes 9437184 | tf_op jit(solution)/shard_map/all_gather | solution.py:44
  18.8 179.0 %all-to-all-start = ((bf16[256,8,1024]{2,0,1:T(8,128)(2,1)}), bf16[256,8,1024]{2,0,1:T(8,128)(2,1)}, u32[]{:S(2)}, u32[]{:S(2)}) async-start(bf16[256,8,1024]{2,0,1:T(8,128)(2,1)} %copy.71), calls=%async_computation | async-start | bytes 8388608 | tf_op jit(solution)/shard_map/all_to_all | solution.py:42
  224.7 218.3 %all-to-all-start.2 = ((bf16[16,64,4,256]{3,2,1,0:T(4,128)(2,1)}), bf16[16,64,4,256]{3,2,1,0:T(4,128)(2,1)}, u32[]{:S(2)}, u32[]{:S(2)}) async-start(bf16[16,64,4,256]{3,2,1,0:T(4,128)(2,1)} %reshape.277), calls=%async_computation.2 | async-start | bytes 4194304 | tf_op jit(solution)/shard_map/all_to_all | solution.py:108
  232.1 10.8 %copy-start.5 = (bf16[2048,1,128]{2,1,0:T(2,128)(2,1)S(1)}, bf16[2048,1,128]{2,1,0:T(2,128)(2,1)}, u32[]{:S(2)}) copy-start(bf16[2048,1,128]{2,1,0:T(2,128)(2,1)} %get-tuple-element.31) | copy-start | bytes 1572868
  233.5 17.5 %copy-start.4 = (bf16[2048,1,128]{2,1,0:T(2,128)(2,1)S(1)}, bf16[2048,1,128]{2,1,0:T(2,128)(2,1)}, u32[]{:S(2)}) copy-start(bf16[2048,1,128]{2,1,0:T(2,128)(2,1)} %get-tuple-element.32) | copy-start | bytes 1572868
  242.8 16.1 %copy-start.3 = (bf16[2048,1,128]{2,1,0:T(2,128)(2,1)S(1)}, bf16[2048,1,128]{2,1,0:T(2,128)(2,1)}, u32[]{:S(2)}) copy-start(bf16[2048,1,128]{2,1,0:T(2,128)(2,1)} %get-tuple-element.33) | copy-start | bytes 1572868
  250.9 16.2 %copy-start.2 = (bf16[2048,1,128]{2,1,0:T(2,128)(2,1)S(1)}, bf16[2048,1,128]{2,1,0:T(2,128)(2,1)}, u32[]{:S(2)}) copy-start(bf16[2048,1,128]{2,1,0:T(2,128)(2,1)} %get-tuple-element.34) | copy-start | bytes 1572868
  278.1 11.3 %copy-start.1 = (f32[2048,2048]{1,0:T(8,128)}, f32[2048,2048]{1,0:T(8,128)S(1)}, u32[]{:S(2)}) copy-start(f32[2048,2048]{1,0:T(8,128)S(1)} %fusion.173) | copy-start | bytes 50331652
  278.1 11.3 %copy-start.6 = (bf16[2048,1,128]{2,1,0:T(2,128)(2,1)S(1)}, bf16[2048,1,128]{2,1,0:T(2,128)(2,1)}, u32[]{:S(2)}) copy-start(bf16[2048,1,128]{2,1,0:T(2,128)(2,1)} %get-tuple-element.30) | copy-start | bytes 1572868
  378.8 17.6 %slice-start.4 = ((s8[16777216]{0:T(1024)(128)(4,1)}), s8[4194304]{0:T(1024)(128)(4,1)S(1)}, s32[]{:S(2)}) async-start(s8[16777216]{0:T(1024)(128)(4,1)} %bitcast.293), calls=%async_computation.8 | async-start | bytes 8388608
  378.8 17.6 %slice-start.5 = ((s8[16777216]{0:T(1024)(128)(4,1)}), s8[4194304]{0:T(1024)(128)(4,1)S(1)}, s32[]{:S(2)}) async-start(s8[16777216]{0:T(1024)(128)(4,1)} %bitcast.293), calls=%async_computation.9 | async-start | bytes 8388608
  387.5 8.8 %slice-start.6 = ((s8[16777216]{0:T(1024)(128)(4,1)}), s8[4194304]{0:T(1024)(128)(4,1)S(1)}, s32[]{:S(2)}) async-start(s8[16777216]{0:T(1024)(128)(4,1)} %bitcast.293), calls=%async_computation.10 | async-start | bytes 8388608
  387.5 8.8 %slice-start.7 = ((s8[16777216]{0:T(1024)(128)(4,1)}), s8[4194304]{0:T(1024)(128)(4,1)S(1)}, s32[]{:S(2)}) async-start(s8[16777216]{0:T(1024)(128)(4,1)} %bitcast.293), calls=%async_computation.11 | async-start | bytes 8388608
  396.3 14.0 %slice-start = ((s8[16777216]{0:T(1024)(128)(4,1)}), s8[4194304]{0:T(1024)(128)(4,1)S(1)}, s32[]{:S(2)}) async-start(s8[16777216]{0:T(1024)(128)(4,1)} %bitcast.291), calls=%async_computation.4 | async-start | bytes 8388608
  396.3 14.0 %slice-start.1 = ((s8[16777216]{0:T(1024)(128)(4,1)}), s8[4194304]{0:T(1024)(128)(4,1)S(1)}, s32[]{:S(2)}) async-start(s8[16777216]{0:T(1024)(128)(4,1)} %bitcast.291), calls=%async_computation.5 | async-start | bytes 8388608
  401.6 8.8 %slice-start.2 = ((s8[16777216]{0:T(1024)(128)(4,1)}), s8[4194304]{0:T(1024)(128)(4,1)S(1)}, s32[]{:S(2)}) async-start(s8[16777216]{0:T(1024)(128)(4,1)} %bitcast.291), calls=%async_computation.6 | async-start | bytes 8388608
  401.6 8.8 %slice-start.3 = ((s8[16777216]{0:T(1024)(128)(4,1)}), s8[4194304]{0:T(1024)(128)(4,1)S(1)}, s32[]{:S(2)}) async-start(s8[16777216]{0:T(1024)(128)(4,1)} %bitcast.291), calls=%async_computation.7 | async-start | bytes 8388608
  410.4 13.8 %slice-start.8 = ((s8[16777216]{0:T(1024)(128)(4,1)}), s8[4194304]{0:T(1024)(128)(4,1)S(1)}, s32[]{:S(2)}) async-start(s8[16777216]{0:T(1024)(128)(4,1)} %bitcast.311), calls=%async_computation.12 | async-start | bytes 8388608
  410.4 13.8 %slice-start.9 = ((s8[16777216]{0:T(1024)(128)(4,1)}), s8[4194304]{0:T(1024)(128)(4,1)S(1)}, s32[]{:S(2)}) async-start(s8[16777216]{0:T(1024)(128)(4,1)} %bitcast.311), calls=%async_computation.13 | async-start | bytes 8388608
  415.5 8.8 %slice-start.10 = ((s8[16777216]{0:T(1024)(128)(4,1)}), s8[4194304]{0:T(1024)(128)(4,1)S(1)}, s32[]{:S(2)}) async-start(s8[16777216]{0:T(1024)(128)(4,1)} %bitcast.311), calls=%async_computation.14 | async-start | bytes 8388608
  415.5 8.8 %slice-start.11 = ((s8[16777216]{0:T(1024)(128)(4,1)}), s8[4194304]{0:T(1024)(128)(4,1)S(1)}, s32[]{:S(2)}) async-start(s8[16777216]{0:T(1024)(128)(4,1)} %bitcast.311), calls=%async_computation.15 | async-start | bytes 8388608
  429.3 19.1 %copy-start.9 = (s32[8,8]{1,0:T(8,128)S(1)}, s32[8,8]{1,0:T(8,128)}, u32[]{:S(2)}) copy-start(s32[8,8]{1,0:T(8,128)} %param.12) | copy-start | bytes 772
  429.3 19.2 %copy-start.8 = (s32[2,512]{1,0:T(2,128)S(1)}, s32[2,512]{1,0:T(2,128)}, u32[]{:S(2)}) copy-start(s32[2,512]{1,0:T(2,128)} %param.14) | copy-start | bytes 12292
  429.3 20.5 %copy-start.10 = (s32[2,512]{1,0:T(2,128)S(1)}, s32[2,512]{1,0:T(2,128)}, u32[]{:S(2)}) copy-start(s32[2,512]{1,0:T(2,128)} %param.15) | copy-start | bytes 12292
  429.3 23.2 %copy-start.11 = (s32[8]{0:T(128)S(1)}, s32[8]{0:T(128)}, u32[]{:S(2)}) copy-start(s32[8]{0:T(128)} %param.13) | copy-start | bytes 100
  443.0 97.1 %all-to-all-start.1 = ((bf16[8,256,1,1024]{3,1,2,0:T(8,128)(2,1)}), bf16[8,256,1,1024]{3,1,2,0:T(8,128)(2,1)}, u32[]{:S(2)}, u32[]{:S(2)}) async-start(bf16[8,256,1,1024]{3,1,2,0:T(8,128)(2,1)} %bitcast.296), calls=%async_computation.1 | async-start | bytes 8388608 | tf_op jit(solution)/shard_map/all_to_all | solution.py:82
Sparse Core Ops, SparseCore 0:
  10.2 203.4 all-gather.2
where the time goes:
time: 570 us; the launch traced here: 560 us
  waiting for transfers between devices  252 us (44%)
  matrix products  168 us (29%)
  local copies, waits for them, and re-layouts  67.9 us (12%)
  other arithmetic  38.9 us (7%)
  starting transfers between devices  18.6 us (3%)
  between operations  14.9 us (3%)
    all_to_all x1, waiting for transfers between devices, on_device(): lax.all_to_all(query_vectors, 'tensor', split_axis=1, concat_axis=0, tile...  172 us
    dot_general x8, matrix products, on_device(): jnp.einsum('rd,nd->rn', own_queries[:, member], key_part, preferred_eleme...  100 us
    all_to_all x1, waiting for transfers between devices, on_device(): lax.all_to_all(attended, 'tensor', split_axis=0, concat_axis=2, tiled=True)  75.4 us
    dot_general x8, matrix products, on_device(): jnp.dot(exp_terms.astype(jnp.bfloat16), value_part, preferred_element_typ...  59 us
    reduce_sum x1, other arithmetic, on_device(): totals = jnp.sum(exp_terms, axis=1, keepdims=True)  35.7 us
    unnamed x53, local copies, waits for them, and re-layouts  17.7 us
  transfers between devices with their start and end apart: 4, of which 3 were waited for; matrix products, arithmetic and copies ran while one was open for 45% of the time, Pallas kernels for 0%

commit v1 on v0

v1 whole, which is shorter than its diff:
```python
import functools
import math

import jax
import jax.numpy as jnp
from jax import lax
from jax.experimental import pallas as pl
from jax.experimental.pallas import tpu as pltpu
from jax.sharding import PartitionSpec as P

QUERY_HEADS = 64
KEY_VALUE_HEADS = 8
HEAD_SIZE = 128
PAGE_TOKENS = 4
GROUP = QUERY_HEADS // KEY_VALUE_HEADS
NEG = -1e30
EXP2_SCALE = math.log2(math.e) / math.sqrt(HEAD_SIZE)
MESH = pl.DeviceIdType.MESH
CHUNK_HEADS = 2
CHUNKS = KEY_VALUE_HEADS // CHUNK_HEADS
HALF = CHUNKS // 2
CHUNK_COLS = CHUNK_HEADS * 2 * HEAD_SIZE


def ring_place(index, n):
    if n != 8:
        return index
    odd = index % 2
    return (index // 2) * (1 - odd) + (n - 1 - index // 2) * odd


def ring_device(place, n):
    place = (place + 2 * n) % n
    if n != 8:
        return place
    far = place // (n // 2)
    return (2 * place) * (1 - far) + (2 * (n - 1 - place) + 1) * far


def scores_t(k, q):
    return lax.dot_general(k, q, (((1,), (1,)), ((), ())), preferred_element_type=jnp.float32)


def flash(s, vt, acc_ref, m_ref, l_ref, h, first):
    top = jnp.max(s, axis=0, keepdims=True)
    if not first:
        old = m_ref[h, 0:1]
        top = jnp.maximum(top, old)
    p = jnp.exp2((s - top) * EXP2_SCALE)
    total = jnp.sum(p, axis=0, keepdims=True)
    mix = jnp.dot(vt, p.astype(jnp.bfloat16), preferred_element_type=jnp.float32)
    if not first:
        alpha = jnp.exp2((old - top) * EXP2_SCALE)
        total = total + l_ref[h, 0:1] * alpha
        mix = mix + acc_ref[h] * alpha
    m_ref[h, 0:1] = top
    l_ref[h, 0:1] = total
    acc_ref[h] = mix


def kernel(
    n,
    q_ref,
    kv_ref,
    pool_ref,
    dq_ref,
    bias_ref,
    old_bias_ref,
    out_ref,
    dec_ref,
    kvs,
    acc,
    m_sc,
    l_sc,
    dacc,
    dm,
    dl,
    dsib,
    dqs,
    xsend,
    xrecv,
    send_sem,
    recv_sem,
    pair_send,
    pair_recv,
):
    rows = q_ref.shape[0]
    steps = dq_ref.shape[1]
    me = lax.axis_index("tensor")
    place = ring_place(me, n)
    right = ring_device(place + 1, n)
    left = ring_device(place - 1, n)
    sibling = 1 - lax.axis_index("section")

    barrier = pltpu.get_barrier_semaphore()
    for target in ({"tensor": right}, {"tensor": left}, {"section": sibling}):
        pl.semaphore_signal(barrier, inc=1, device_id=target, device_id_type=MESH)
    pl.semaphore_wait(barrier, 3)

    def ring_copy(src, slot, chunk, step, target):
        return pltpu.make_async_remote_copy(
            src_ref=src,
            dst_ref=kvs.at[slot, chunk],
            send_sem=send_sem.at[step * CHUNKS + chunk],
            recv_sem=recv_sem.at[step * CHUNKS + chunk],
            device_id={"tensor": target},
            device_id_type=MESH,
        )

    def pair_copy(src, dst, which):
        return pltpu.make_async_remote_copy(
            src_ref=src,
            dst_ref=dst,
            send_sem=pair_send.at[which],
            recv_sem=pair_recv.at[which],
            device_id={"section": sibling},
            device_id_type=MESH,
        )

    for c in range(HALF):
        for chunk, target in ((c, right), (HALF + c, left)):
            kvs[me, chunk] = kv_ref[:, chunk * CHUNK_COLS : (chunk + 1) * CHUNK_COLS]
            ring_copy(kvs.at[me, chunk], me, chunk, 0, target).start()
    swap_queries = pair_copy(dq_ref, dsib, 0)
    swap_queries.start()

    causal = lax.broadcasted_iota(jnp.int32, (rows, rows), 1) >= lax.broadcasted_iota(
        jnp.int32, (rows, rows), 0
    )

    def query_head(h):
        return q_ref[:, pl.ds(pl.multiple_of(h * HEAD_SIZE, HEAD_SIZE), HEAD_SIZE)]

    def attend(k, vt, g, first):
        s = scores_t(k, query_head(g * GROUP))
        for j in range(GROUP):
            following = scores_t(k, query_head(g * GROUP + j + 1)) if j + 1 < GROUP else None
            if first:
                s = jnp.where(causal, s, NEG)
            flash(s, vt, acc, m_sc, l_sc, g * GROUP + j, first)
            s = following

    def kv_cols(ref, g):
        start = pl.multiple_of(g * 2 * HEAD_SIZE, 2 * HEAD_SIZE)
        return (
            ref[:, pl.ds(start, HEAD_SIZE)],
            ref[:, pl.ds(pl.multiple_of(start + HEAD_SIZE, HEAD_SIZE), HEAD_SIZE)],
        )

    swap_queries.wait()
    for g in range(KEY_VALUE_HEADS):
        dqs[g, 0:steps] = dq_ref[g]
        dqs[g, steps : 2 * steps] = dsib[g]
        start = g * 2 * HEAD_SIZE
        k = pool_ref[:, start : start + HEAD_SIZE]
        v = pool_ref[:, start + HEAD_SIZE : start + 2 * HEAD_SIZE]
        s = scores_t(k, dqs[g]) + old_bias_ref[...]
        flash(s, jnp.transpose(v), dacc, dm, dl, g, True)

    def own_head(g, carry):
        k, v = kv_cols(kv_ref, g)
        vt = jnp.transpose(v)
        s = scores_t(k, dqs[g]) + bias_ref[me]
        flash(s, vt, dacc, dm, dl, g, False)
        attend(k, vt, g, True)
        return carry

    lax.fori_loop(0, KEY_VALUE_HEADS, own_head, 0)

    def ring_step(step, carry):
        src_right = ring_device(place - step, n)
        src_left = ring_device(place + step, n)

        def part(c, carry):
            for chunk, slot, target in ((c, src_right, right), (HALF + c, src_left, left)):
                block = kvs.at[slot, chunk]
                ring_copy(block, slot, chunk, step - 1, target).wait_recv()

                @pl.when(step < n - 1)
                def _():
                    ring_copy(block, slot, chunk, step, target).start()

            def unit(u, carry):
                way = u // CHUNK_HEADS
                inner = u % CHUNK_HEADS
                chunk = way * HALF + c
                slot = src_right * (1 - way) + src_left * way
                g = chunk * CHUNK_HEADS + inner
                start = pl.multiple_of(inner * 2 * HEAD_SIZE, 2 * HEAD_SIZE)
                k = kvs[slot, chunk, :, pl.ds(start, HEAD_SIZE)]
                v = kvs[
                    slot, chunk, :, pl.ds(pl.multiple_of(start + HEAD_SIZE, HEAD_SIZE), HEAD_SIZE)
                ]
                vt = jnp.transpose(v)
                s = scores_t(k, dqs[g]) + bias_ref[slot]
                flash(s, vt, dacc, dm, dl, g, False)

                @pl.when(slot < me)
                def _():
                    attend(k, vt, g, False)

                return carry

            return lax.fori_loop(0, 2 * CHUNK_HEADS, unit, carry)

        return lax.fori_loop(0, HALF, part, carry)

    lax.fori_loop(1, n, ring_step, 0)

    def columns(row):
        return jnp.transpose(jnp.broadcast_to(row, (HEAD_SIZE, 2 * steps)))

    def stage(g, carry):
        xsend[g, 0] = jnp.transpose(dacc[g])[steps:]
        xsend[g, 1] = columns(dm[g, 0:1])[steps:]
        xsend[g, 2] = columns(dl[g, 0:1])[steps:]
        return carry

    lax.fori_loop(0, KEY_VALUE_HEADS, stage, 0)
    swap_parts = pair_copy(xsend, xrecv, 1)
    swap_parts.start()

    def finish(h, carry):
        mix = acc[h] / l_sc[h, 0:1]
        out_ref[:, pl.ds(pl.multiple_of(h * HEAD_SIZE, HEAD_SIZE), HEAD_SIZE)] = jnp.transpose(
            mix
        ).astype(jnp.bfloat16)
        return carry

    lax.fori_loop(0, QUERY_HEADS, finish, 0)
    swap_parts.wait()
    trajs = steps // GROUP
    for g in range(KEY_VALUE_HEADS):
        o_own = jnp.transpose(dacc[g])[:steps]
        m_own = columns(dm[g, 0:1])[:steps]
        l_own = columns(dl[g, 0:1])[:steps]
        top = jnp.maximum(m_own, xrecv[g, 1])
        w_own = jnp.exp2((m_own - top) * EXP2_SCALE)
        w_sib = jnp.exp2((xrecv[g, 1] - top) * EXP2_SCALE)
        mix = (o_own * w_own + xrecv[g, 0] * w_sib) / (l_own * w_own + xrecv[g, 2] * w_sib)
        for j in range(GROUP):
            col = (g * GROUP + j) * HEAD_SIZE
            dec_ref[:, col : col + HEAD_SIZE] = mix[j * trajs : (j + 1) * trajs].astype(
                jnp.bfloat16
            )

    def drain(step, carry):
        for c in range(HALF):
            for chunk, target in ((c, right), (HALF + c, left)):
                ring_copy(kvs.at[me, chunk], me, chunk, step, target).wait_send()
        return carry

    lax.fori_loop(0, n - 1, drain, 0)


def on_device(
    prefill_queries,
    prefill_key_values,
    decode_step_queries,
    cached_page_pool,
    trajectory_page_table,
    lengths,
    page_owner,
    page_slot,
):
    n = lax.axis_size("tensor")
    sections = lax.axis_size("section")
    me = lax.axis_index("tensor")
    section = lax.axis_index("section")
    rows = prefill_queries.shape[1]
    trajs = decode_step_queries.shape[0]
    steps = trajs * GROUP
    old_rows = cached_page_pool.shape[0] * PAGE_TOKENS
    q = prefill_queries[0]
    kv = prefill_key_values[0]
    pool = cached_page_pool.reshape(old_rows, cached_page_pool.shape[2])
    dq = (
        decode_step_queries.reshape(trajs, KEY_VALUE_HEADS, GROUP, HEAD_SIZE)
        .transpose(1, 2, 0, 3)
        .reshape(KEY_VALUE_HEADS, steps, HEAD_SIZE)
    )
    lanes = jnp.arange(2 * steps, dtype=jnp.int32)
    lane_traj = lanes % trajs
    lane_owner = me * sections + jnp.where(lanes < steps, section, 1 - section)
    target = lax.dynamic_index_in_dim(page_owner * trajs + page_slot, section, 0, keepdims=False)
    target = jnp.repeat(target, PAGE_TOKENS)
    bias = jnp.where(
        target[:, None] == (lane_owner * trajs + lane_traj)[None, :], 0.0, NEG
    ).astype(jnp.float32)
    bias = bias.reshape(n, rows, 2 * steps)
    slots = cached_page_pool.shape[0]
    pages = trajectory_page_table.shape[1]
    named = trajectory_page_table[None] == jnp.arange(slots, dtype=jnp.int32)[:, None, None]
    left_tokens = lengths[:, None] - jnp.arange(pages, dtype=jnp.int32)[None, :] * PAGE_TOKENS
    count = jnp.sum(jnp.where(named, left_tokens[None], 0), axis=2)
    count_rows = jnp.repeat(count, PAGE_TOKENS, axis=0)
    within = jnp.arange(old_rows, dtype=jnp.int32) % PAGE_TOKENS
    valid = within[:, None] < count_rows
    old_bias = jnp.where(jnp.tile(valid, (1, 2 * GROUP)) & (lanes < steps)[None, :], 0.0, NEG)
    old_bias = old_bias.astype(jnp.float32)

    vmem = pl.BlockSpec(memory_space=pltpu.VMEM)
    f32 = jnp.float32
    out, dec = pl.pallas_call(
        functools.partial(kernel, n),
        out_shape=(
            jax.ShapeDtypeStruct((rows, QUERY_HEADS * HEAD_SIZE), jnp.bfloat16),
            jax.ShapeDtypeStruct((trajs, QUERY_HEADS * HEAD_SIZE), jnp.bfloat16),
        ),
        in_specs=[vmem] * 6,
        out_specs=(vmem, vmem),
        scratch_shapes=[
            pltpu.VMEM((n, CHUNKS, rows, CHUNK_COLS), jnp.bfloat16),
            pltpu.VMEM((QUERY_HEADS, HEAD_SIZE, rows), f32),
            pltpu.VMEM((QUERY_HEADS, 8, rows), f32),
            pltpu.VMEM((QUERY_HEADS, 8, rows), f32),
            pltpu.VMEM((KEY_VALUE_HEADS, HEAD_SIZE, 2 * steps), f32),
            pltpu.VMEM((KEY_VALUE_HEADS, 8, 2 * steps), f32),
            pltpu.VMEM((KEY_VALUE_HEADS, 8, 2 * steps), f32),
            pltpu.VMEM((KEY_VALUE_HEADS, steps, HEAD_SIZE), jnp.bfloat16),
            pltpu.VMEM((KEY_VALUE_HEADS, 2 * steps, HEAD_SIZE), jnp.bfloat16),
            pltpu.VMEM((KEY_VALUE_HEADS, 3, steps, HEAD_SIZE), f32),
            pltpu.VMEM((KEY_VALUE_HEADS, 3, steps, HEAD_SIZE), f32),
            pltpu.SemaphoreType.DMA(((n - 1) * CHUNKS,)),
            pltpu.SemaphoreType.DMA(((n - 1) * CHUNKS,)),
            pltpu.SemaphoreType.DMA((2,)),
            pltpu.SemaphoreType.DMA((2,)),
        ],
        compiler_params=pltpu.CompilerParams(
            collective_id=0, has_side_effects=True, vmem_limit_bytes=44 * 1024 * 1024
        ),
    )(q, kv, pool, dq, bias, old_bias)
    return (out[None], dec)


def solution(mesh):
    placed = (
        P("section", ("groups", "tensor"), None),
        P("section", ("groups", "tensor"), None),
        P(("groups", "tensor", "section"), None),
        P(("groups", "tensor", "section"), None, None),
        P(("groups", "tensor", "section"), None),
        P(("groups", "tensor", "section")),
        P(None, "groups"),
        P(None, "groups"),
    )
    return jax.shard_map(
        on_device,
        mesh=mesh,
        in_specs=placed,
        out_specs=(
            P("section", ("groups", "tensor"), None),
            P(("groups", "tensor", "section"), None),
        ),
        check_vma=False,
    )
```

time: 570 us -> 140 us (0.25); the launches traced: 560 us -> 139 us
  waiting for transfers between devices: 252 us -> 0 us
  matrix products: 168 us -> 0 us
  Pallas kernels: 0 us -> 131 us
  local copies, waits for them, and re-layouts: 67.9 us -> 4.59 us
  other arithmetic: 38.9 us -> 2.79 us
  starting transfers between devices: 18.6 us -> 0 us
  between operations: 14.9 us -> 0.77 us
    all_to_all x3 -> x0, waiting for transfers between devices: 247 us -> none  [the longest x1 172 us: on_device(): lax.all_to_all(query_vectors, 'tensor', split_axis=1, concat_axis=0, tile...]
    dot_general x21 -> x0, matrix products: 168 us -> none  [the longest x8 100 us: on_device(): jnp.einsum('rd,nd->rn', own_queries[:, member], key_part, preferred_eleme...]
    pallas_call x0 -> x1, Pallas kernels: none -> 131 us  [on_device(): pl.pallas_call(functools.partial(kernel, n), out_shape=(jax.ShapeDtypeStr...]
    reduce_sum x5 -> x1, other arithmetic: 36.5 us -> 0.78 us  [on_device(): count = jnp.sum(jnp.where(named, left_tokens[None], 0), axis=2)]
    all_to_all x3 -> x0, starting transfers between devices: 18.5 us -> none  [the longest x1 7.39 us: on_device(): lax.all_to_all(outgoing, ('tensor', 'section'), split_axis=0, concat_axis...]
    unnamed x53 -> x6, local copies, waits for them, and re-layouts: 17.7 us -> 2.68 us
    reshape x7 -> x1, local copies, waits for them, and re-layouts: 14.7 us -> 1.34 us  [on_device(): pool = cached_page_pool.reshape(old_rows, cached_page_pool.shape[2])]
    slice x3 -> x0, local copies, waits for them, and re-layouts: 10.7 us -> none  [the longest x1 8.15 us: on_device(): own_queries[:, member]]
  transfers between devices with their start and end apart: 4 -> 0, of which waited for: 3 -> 0; matrix products, arithmetic and copies ran while one was open for 45% -> 0% of each run, Pallas kernels for 0% -> 0%
where the time goes in v1:
time: 140 us; the launch traced here: 139 us
  Pallas kernels  131 us (94%)
  local copies, waits for them, and re-layouts  4.59 us (3%)
  other arithmetic  2.79 us (2%)
    pallas_call x1, Pallas kernels, on_device(): pl.pallas_call(functools.partial(kernel, n), out_shape=(jax.ShapeDtypeStr...  131 us

profile of v1, /device:TPU:29, one launch (start us, length us, event | category | flops | bytes accessed | tf_op | source)
XLA Modules:
  0.0 139.4 jit_solution(12360065321581873267)
XLA Ops:
  0.6 0.0 copy-start.1
  0.6 0.0 copy-start
  0.7 0.8 fusion
  1.5 0.1 broadcast_in_dim.57
  1.6 0.7 broadcast_subtract_fusion
  2.3 0.8 select_reduce_fusion
  3.1 0.1 copy.18
  3.2 0.1 copy.16
  3.3 0.1 copy.17
  3.4 0.1 broadcast_compare_fusion
  3.5 0.1 copy.19
  3.6 0.1 copy.20
  3.8 0.3 compare_select_fusion.bias_ref
  4.1 1.3 reshape.108.pool_ref
  5.5 0.0 copy-done.1
  5.5 0.0 copy-done
  5.5 131.2 %shard_map.95 = (bf16[256,8192]{1,0:T(8,128)(2,1)S(1)}, bf16[8,8192]{1,0:T(8,128)(2,1)S(1)}) custom-call(bf16[256,8192]{1,0:T(8,128)(2,1)} %bitcast.15, bf16[256,2048]{1,0:T(8,128)(2,1)S(1)} %bitcast.13, bf16[256,2048]{1,0:T(8,128)(2,1)S(1)} %reshape.108.pool_ref, bf16[8,64,128]{2,1,0:T(8,128)(2,1)S(1)} %bitcast.14, ...), custom_call_target="tpu_custom_call" | custom-call | tf_op jit(solution)/shard_map/pallas_call | solution.py:304
  136.7 2.0 %copy.23 = bf16[1,256,8192]{2,1,0:T(8,128)(2,1)} copy(bf16[1,256,8192]{2,1,0:T(8,128)(2,1)S(1)} %bitcast.12) | data formatting | bytes 8388608
  138.7 0.7 copy.24
  (8 shorter events, 0.1 us)
Async XLA Ops:
  0.6 4.8 %copy-start.1 = (bf16[8,8192]{1,0:T(8,128)(2,1)S(1)}, bf16[8,8192]{1,0:T(8,128)(2,1)}, u32[]{:S(2)}) copy-start(bf16[8,8192]{1,0:T(8,128)(2,1)} %param.10) | copy-start | bytes 393220
  0.6 4.8 %copy-start = (bf16[1,256,2048]{2,1,0:T(8,128)(2,1)S(1)}, bf16[1,256,2048]{2,1,0:T(8,128)(2,1)}, u32[]{:S(2)}) copy-start(bf16[1,256,2048]{2,1,0:T(8,128)(2,1)} %param.9) | copy-start | bytes 3145732

commit v2 on v1

--- a/solution.py
+++ b/solution.py
@@ -13,6 +13,7 @@
 HEAD_SIZE = 128
 PAGE_TOKENS = 4
 GROUP = QUERY_HEADS // KEY_VALUE_HEADS
+BATCH = 4
 NEG = -1e30
 EXP2_SCALE = math.log2(math.e) / math.sqrt(HEAD_SIZE)
 MESH = pl.DeviceIdType.MESH
@@ -41,21 +42,28 @@
     return lax.dot_general(k, q, (((1,), (1,)), ((), ())), preferred_element_type=jnp.float32)
 
 
-def flash(s, vt, acc_ref, m_ref, l_ref, h, first):
-    top = jnp.max(s, axis=0, keepdims=True)
-    if not first:
-        old = m_ref[h, 0:1]
-        top = jnp.maximum(top, old)
-    p = jnp.exp2((s - top) * EXP2_SCALE)
-    total = jnp.sum(p, axis=0, keepdims=True)
-    mix = jnp.dot(vt, p.astype(jnp.bfloat16), preferred_element_type=jnp.float32)
-    if not first:
-        alpha = jnp.exp2((old - top) * EXP2_SCALE)
-        total = total + l_ref[h, 0:1] * alpha
-        mix = mix + acc_ref[h] * alpha
-    m_ref[h, 0:1] = top
-    l_ref[h, 0:1] = total
-    acc_ref[h] = mix
+def flash(parts, acc_ref, m_ref, l_ref, first):
+    tops, alphas, totals, probs = [], [], [], []
+    for s, _, h in parts:
+        top = jnp.max(s, axis=0, keepdims=True)
+        if not first:
+            old = m_ref[h, 0:1]
+            top = jnp.maximum(top, old)
+            alphas.append(jnp.exp2((old - top) * EXP2_SCALE))
+        tops.append(top)
+    for i, (s, _, h) in enumerate(parts):
+        p = jnp.exp2((s - tops[i]) * EXP2_SCALE)
+        total = jnp.sum(p, axis=0, keepdims=True)
+        totals.append(total if first else total + l_ref[h, 0:1] * alphas[i])
+        probs.append(p.astype(jnp.bfloat16))
+    mixes = []
+    for i, (_, vt, h) in enumerate(parts):
+        mix = jnp.dot(vt, probs[i], preferred_element_type=jnp.float32)
+        mixes.append(mix if first else mix + acc_ref[h] * alphas[i])
+    for i, (_, _, h) in enumerate(parts):
+        m_ref[h, 0:1] = tops[i]
+        l_ref[h, 0:1] = totals[i]
+        acc_ref[h] = mixes[i]
 
 
 def kernel(
@@ -132,13 +140,14 @@
         return q_ref[:, pl.ds(pl.multiple_of(h * HEAD_SIZE, HEAD_SIZE), HEAD_SIZE)]
 
     def attend(k, vt, g, first):
-        s = scores_t(k, query_head(g * GROUP))
-        for j in range(GROUP):
-            following = scores_t(k, query_head(g * GROUP + j + 1)) if j + 1 < GROUP else None
-            if first:
-                s = jnp.where(causal, s, NEG)
-            flash(s, vt, acc, m_sc, l_sc, g * GROUP + j, first)
-            s = following
+        for start in range(0, GROUP, BATCH):
+            parts = []
+            for j in range(start, start + BATCH):
+                s = scores_t(k, query_head(g * GROUP + j))
+                if first:
+                    s = jnp.where(causal, s, NEG)
+                parts.append((s, vt, g * GROUP + j))
+            flash(parts, acc, m_sc, l_sc, first)
 
     def kv_cols(ref, g):
         start = pl.multiple_of(g * 2 * HEAD_SIZE, 2 * HEAD_SIZE)
@@ -148,6 +157,7 @@
         )
 
     swap_queries.wait()
+    pool_parts = []
     for g in range(KEY_VALUE_HEADS):
         dqs[g, 0:steps] = dq_ref[g]
         dqs[g, steps : 2 * steps] = dsib[g]
@@ -155,13 +165,16 @@
         k = pool_ref[:, start : start + HEAD_SIZE]
         v = pool_ref[:, start + HEAD_SIZE : start + 2 * HEAD_SIZE]
         s = scores_t(k, dqs[g]) + old_bias_ref[...]
-        flash(s, jnp.transpose(v), dacc, dm, dl, g, True)
+        pool_parts.append((s, jnp.transpose(v), g))
+
+    for g in range(0, KEY_VALUE_HEADS, HALF):
+        flash(pool_parts[g : g + HALF], dacc, dm, dl, True)
 
     def own_head(g, carry):
         k, v = kv_cols(kv_ref, g)
         vt = jnp.transpose(v)
         s = scores_t(k, dqs[g]) + bias_ref[me]
-        flash(s, vt, dacc, dm, dl, g, False)
+        flash([(s, vt, g)], dacc, dm, dl, False)
         attend(k, vt, g, True)
         return carry
 
@@ -179,6 +192,18 @@
                 @pl.when(step < n - 1)
                 def _():
                     ring_copy(block, slot, chunk, step, target).start()
+
+            parts = []
+            for way, slot in ((0, src_right), (1, src_left)):
+                mask = bias_ref[slot]
+                for inner in range(CHUNK_HEADS):
+                    chunk = way * HALF + c
+                    start = inner * 2 * HEAD_SIZE
+                    k = kvs[slot, chunk, :, start : start + HEAD_SIZE]
+                    v = kvs[slot, chunk, :, start + HEAD_SIZE : start + 2 * HEAD_SIZE]
+                    g = chunk * CHUNK_HEADS + inner
+                    parts.append((scores_t(k, dqs[g]) + mask, jnp.transpose(v), g))
+            flash(parts, dacc, dm, dl, False)
 
             def unit(u, carry):
                 way = u // CHUNK_HEADS
@@ -192,12 +217,12 @@
                     slot, chunk, :, pl.ds(pl.multiple_of(start + HEAD_SIZE, HEAD_SIZE), HEAD_SIZE)
                 ]
                 vt = jnp.transpose(v)
-                s = scores_t(k, dqs[g]) + bias_ref[slot]
-                flash(s, vt, dacc, dm, dl, g, False)
-
                 @pl.when(slot < me)
                 def _():
-                    attend(k, vt, g, False)
+                    k = kvs[slot, chunk, :, pl.ds(start, HEAD_SIZE)]
+                    after = pl.multiple_of(start + HEAD_SIZE, HEAD_SIZE)
+                    v = kvs[slot, chunk, :, pl.ds(after, HEAD_SIZE)]
+                    attend(k, jnp.transpose(v), g, False)
 
                 return carry
 

time: 140 us -> 107 us (0.76)
  Pallas kernels: 131 us -> 98.1 us
    pallas_call x1, Pallas kernels: 131 us -> 98.1 us  [on_device(): pl.pallas_call(functools.partial(kernel, n), out_shape=(jax.ShapeDtypeStr...]
where the time goes in v2:
time: 107 us; the launch traced here: 106 us
  Pallas kernels  98.1 us (92%)
  local copies, waits for them, and re-layouts  4.59 us (4%)
  other arithmetic  2.79 us (3%)
    pallas_call x1, Pallas kernels, on_device(): pl.pallas_call(functools.partial(kernel, n), out_shape=(jax.ShapeDtypeStr...  98.1 us
    unnamed x6, local copies, waits for them, and re-layouts  2.68 us

profile of v2, /device:TPU:29, one launch (start us, length us, event | category | flops | bytes accessed | tf_op | source)
XLA Modules:
  0.0 106.2 jit_solution(11559415488316999124)
XLA Ops:
  0.6 0.0 copy-start.1
  0.6 0.0 copy-start
  0.7 0.8 fusion
  1.5 0.1 broadcast_in_dim.57
  1.6 0.7 broadcast_subtract_fusion
  2.3 0.8 select_reduce_fusion
  3.1 0.1 copy.18
  3.2 0.1 copy.16
  3.3 0.1 copy.17
  3.4 0.1 broadcast_compare_fusion
  3.5 0.1 copy.19
  3.6 0.1 copy.20
  3.8 0.3 compare_select_fusion.bias_ref
  4.1 1.3 %reshape.108.pool_ref = bf16[256,2048]{1,0:T(8,128)(2,1)S(1)} reshape(bf16[64,4,2048]{2,1,0:T(4,128)(2,1)} %param.11) | data formatting | bytes 2097152 | tf_op jit(solution)/shard_map/reshape | solution.py:301
  5.5 0.0 copy-done.1
  5.5 0.0 copy-done
  5.5 98.1 %shard_map.95 = (bf16[256,8192]{1,0:T(8,128)(2,1)S(1)}, bf16[8,8192]{1,0:T(8,128)(2,1)S(1)}) custom-call(bf16[256,8192]{1,0:T(8,128)(2,1)} %bitcast.15, bf16[256,2048]{1,0:T(8,128)(2,1)S(1)} %bitcast.13, bf16[256,2048]{1,0:T(8,128)(2,1)S(1)} %reshape.108.pool_ref, bf16[8,64,128]{2,1,0:T(8,128)(2,1)S(1)} %bitcast.14, ...), custom_call_target="tpu_custom_call" | custom-call | tf_op jit(solution)/shard_map/pallas_call | solution.py:329
  103.5 2.0 %copy.23 = bf16[1,256,8192]{2,1,0:T(8,128)(2,1)} copy(bf16[1,256,8192]{2,1,0:T(8,128)(2,1)S(1)} %bitcast.12) | data formatting | bytes 8388608
  105.6 0.7 copy.24
  (8 shorter events, 0.1 us)
Async XLA Ops:
  0.6 4.8 %copy-start.1 = (bf16[8,8192]{1,0:T(8,128)(2,1)S(1)}, bf16[8,8192]{1,0:T(8,128)(2,1)}, u32[]{:S(2)}) copy-start(bf16[8,8192]{1,0:T(8,128)(2,1)} %param.10) | copy-start | bytes 393220
  0.6 4.8 %copy-start = (bf16[1,256,2048]{2,1,0:T(8,128)(2,1)S(1)}, bf16[1,256,2048]{2,1,0:T(8,128)(2,1)}, u32[]{:S(2)}) copy-start(bf16[1,256,2048]{2,1,0:T(8,128)(2,1)} %param.9) | copy-start | bytes 3145732
